TPU v7x, 512 devices: a whole 4x4x16 slice. The times are simulated.
512 devices in a mesh: tile: 32 (over z, core), band: 4 (over x), pos: 4 (over y).
Axes of the slice: x: 4, y: 4, z: 16, core: 2. Of those that a mesh axis runs over, the one named last changes fastest.
Arguments:
- object_planes: float32 [2, 8192, 1024], P(None, 'tile', 'band'), may hold values from -6 to 6
- probe_planes: float32 [2, 2, 256, 256], replicated, may hold values from -6 to 6
- patterns: float32 [32, 4, 4, 3, 256, 256], P('tile', 'band', 'pos'), may hold values from 0.5 to 8
- offsets: int32 [32, 4, 4, 3, 2], P('tile', 'band', 'pos'), may hold values from 0 to 255, as said below
- counts: int32 [32, 4, 4], P('tile', 'band', 'pos'), may hold values from 0 to 3, as said below
Outputs:
- object_new: float32 [2, 8192, 1024], P(None, 'tile', 'band')
- probe_new: float32 [2, 2, 256, 256], replicated
Inputs may be any that keep to these rules, and one draw needn't show every extreme that they name: `offsets`: corners lie inside their tile: rows below 256, columns below 256. Only the first counts[t, b, p] slots of a device hold positions; later slots are to be ignored. `counts`: each device holds at most 3 positions; in every tile one device along pos holds exactly 3, and the 4 devices of a tile hold exactly 8 positions together.
All inputs are finite; a program needn't handle non-finite values.
Results may differ from a plain program's by a relative error of at most 0.0003.
Values sent between devices are 32-bit elements; how exact they have to be, the bound alone decides.
No kernel may reach another device: no remote copies, remote signals or barrier semaphores. Data moves between devices by JAX's collectives and lax.ppermute only.
A program may use at most 192 MiB of HBM per device.

v0:
```python
import math
import jax
import jax.numpy as jnp
from jax import lax
from jax.sharding import PartitionSpec as P

precise = lax.Precision.HIGHEST


def shifted(block, axis, distance):
    devices = range(lax.axis_size(axis))
    route = [(i - distance, i) for i in devices if i - distance in devices]
    return lax.ppermute(block, axis, route)


def dft_tables(pixels):
    indices = jnp.arange(pixels, dtype=jnp.int32)
    phase = indices[:, None] * indices[None, :] % pixels
    angle = phase.astype(jnp.float32) * (2.0 * math.pi / pixels)
    factor = 1.0 / math.sqrt(pixels)
    return (jnp.cos(angle) * factor, jnp.sin(angle) * factor)


def transform(real_part, imag_part, cosine, sine_table, direction):
    left_real = jnp.einsum(
        "ij,nmjk->nmik", cosine, real_part, precision=precise
    ) + direction * jnp.einsum("ij,nmjk->nmik", sine_table, imag_part, precision=precise)
    left_imag = jnp.einsum(
        "ij,nmjk->nmik", cosine, imag_part, precision=precise
    ) - direction * jnp.einsum("ij,nmjk->nmik", sine_table, real_part, precision=precise)
    out_real = jnp.einsum(
        "nmij,jk->nmik", left_real, cosine, precision=precise
    ) + direction * jnp.einsum("nmij,jk->nmik", left_imag, sine_table, precision=precise)
    out_imag = jnp.einsum(
        "nmij,jk->nmik", left_imag, cosine, precision=precise
    ) - direction * jnp.einsum("nmij,jk->nmik", left_real, sine_table, precision=precise)
    return (out_real, out_imag)


def on_device(object_planes, probe_planes, patterns, offsets, counts):
    pixels = probe_planes.shape[-1]
    capacity = patterns.shape[3]
    tile_rows = object_planes.shape[1]
    tile_cols = object_planes.shape[2]
    beside_cols = shifted(object_planes, "band", -1)
    widened = jnp.concatenate([object_planes, beside_cols], axis=2)
    below_rows = shifted(widened, "tile", -1)
    extended = jnp.concatenate([widened, below_rows], axis=1)
    local_count = counts.reshape(())
    frames = patterns[0, 0, 0]
    places = offsets[0, 0, 0]
    weights = (jnp.arange(capacity, dtype=jnp.int32) < local_count).astype(jnp.float32)
    slot_total = frames.shape[0]
    zero_index = jnp.int32(0)
    patches = jnp.stack(
        [
            lax.dynamic_slice(
                extended, (zero_index, places[number, 0], places[number, 1]), (2, pixels, pixels)
            )
            for number in range(slot_total)
        ]
    )
    patch_real = patches[:, 0][:, None]
    patch_imag = patches[:, 1][:, None]
    probe_real = probe_planes[0][None]
    probe_imag = probe_planes[1][None]
    wave_real = probe_real * patch_real - probe_imag * patch_imag
    wave_imag = probe_real * patch_imag + probe_imag * patch_real
    cosine, sine_table = dft_tables(pixels)
    far_real, far_imag = transform(wave_real, wave_imag, cosine, sine_table, 1.0)
    intensity = jnp.sum(far_real * far_real + far_imag * far_imag, axis=1)
    scaling = (jnp.sqrt(frames) / jnp.sqrt(intensity + 1.0))[:, None]
    back_real, back_imag = transform(
        far_real * scaling, far_imag * scaling, cosine, sine_table, -1.0
    )
    corr_real = back_real - wave_real
    corr_imag = back_imag - wave_imag
    slot_weight = weights[:, None, None]
    object_real = slot_weight * jnp.sum(probe_real * corr_real + probe_imag * corr_imag, axis=1)
    object_imag = slot_weight * jnp.sum(probe_real * corr_imag - probe_imag * corr_real, axis=1)
    probe_power = jnp.sum(probe_planes[0] ** 2 + probe_planes[1] ** 2, axis=0)
    lighting = slot_weight * probe_power[None]
    contributions = jnp.stack([object_real, object_imag, lighting], axis=1)
    plane_count = contributions.shape[1]
    running = jnp.zeros((plane_count, tile_rows + pixels, tile_cols + pixels), jnp.float32)
    for number in range(slot_total):
        corner_at = (zero_index, places[number, 0], places[number, 1])
        previous = lax.dynamic_slice(running, corner_at, (plane_count, pixels, pixels))
        running = lax.dynamic_update_slice(running, previous + contributions[number], corner_at)
    mode_weight = weights[:, None, None, None]
    numer_real = jnp.sum(mode_weight * (patch_real * corr_real + patch_imag * corr_imag), axis=0)
    numer_imag = jnp.sum(mode_weight * (patch_real * corr_imag - patch_imag * corr_real), axis=0)
    density = jnp.sum(slot_weight * (patches[:, 0] ** 2 + patches[:, 1] ** 2), axis=0)
    from_left = shifted(running[:, :, tile_cols:], "band", 1)
    column_core = running[:, :, :tile_cols].at[:, :, :pixels].add(from_left)
    from_above = shifted(column_core[:, tile_rows:, :], "tile", 1)
    tile_core = column_core[:, :tile_rows, :].at[:, :pixels, :].add(from_above)
    tile_total = lax.psum(tile_core, "pos")
    tile_light = tile_total[2]
    object_new = object_planes + tile_total[:2] / (tile_light + 1.0)
    sum_numer, sum_density = lax.psum(
        (jnp.stack([numer_real, numer_imag]), density), ("tile", "band", "pos")
    )
    probe_new = probe_planes + sum_numer / (sum_density + 1.0)
    return (object_new, probe_new)


def solution(mesh):
    in_specs = (
        P(None, "tile", "band"),
        P(),
        P("tile", "band", "pos", None, None, None),
        P("tile", "band", "pos", None, None),
        P("tile", "band", "pos"),
    )
    out_specs = (P(None, "tile", "band"), P())
    return jax.shard_map(
        on_device, mesh=mesh, in_specs=in_specs, out_specs=out_specs, check_vma=False
    )
```

profile of v0, /device:TPU:2, one launch (start us, length us, event | category | flops | bytes accessed | tf_op | source)
XLA Modules:
  0.0 733.1 jit_solution(11217168582069033955)
XLA Ops:
  7.2 0.0 copy-start.2
  7.2 0.0 all-reduce.6.cloned.1.call-start
  7.2 8.0 %collective-permute-start = (f32[2,256,256]{2,1,0:T(8,128)}, f32[2,256,256]{2,1,0:T(8,128)S(1)}, u32[]{:S(2)}, u32[]{:S(2)}) collective-permute-start(f32[2,256,256]{2,1,0:T(8,128)} %param.13), channel_id=1, source_target_pairs={{4,0},{8,4},{12,8},{5,1},{9,5},{13,9},{6,2},{10,6},{14,10},{7,3},{... | collective-permute-start | bytes 1572872 | tf_op jit(solution)/shard_map/ppermute | solution.py:13
  15.2 1.1 constant_dynamic-update-slice_fusion.1
  16.3 6.8 collective-permute-done
  23.1 0.1 constant_dynamic-update-slice_fusion
  23.2 1.3 collective-permute-start.1
  24.5 0.6 fusion.170
  37.1 0.1 add_reduce_fusion.2
  37.2 0.1 slice_bitcast_fusion.6
  37.3 0.0 collective-permute-done.1
  37.3 1.0 fusion.63
  38.2 0.1 pad_maximum_fusion.1
  38.4 0.1 slice_bitcast_fusion.4
  38.5 1.0 copy-done
  39.5 3.7 fusion.16
  43.2 3.7 fusion.31
  46.9 4.1 fusion.8
  51.0 3.6 fusion.10
  54.6 3.7 fusion.17
  58.3 3.7 fusion.30
  62.0 3.8 fusion.20
  65.8 0.0 copy-start.7
  65.9 3.8 add_reduce_fusion.1
  69.6 0.3 bitcast_multiply_fusion.2
  69.9 3.6 fusion.36
  73.5 3.8 fusion.32
  77.3 3.6 multiply_subtract_fusion
  80.9 3.6 fusion
  84.6 4.0 fusion.2
  88.6 3.6 multiply_add_fusion
  92.2 3.9 add_subtract_fusion
  96.2 6.0 multiply_reduce_fusion.1
  102.1 0.3 bitcast_multiply_fusion.1
  102.4 0.2 pad_maximum_fusion
  102.6 1.0 slice_bitcast_fusion.2
  103.6 0.7 copy-done.4
  104.3 0.4 broadcast_in_dim.2
  104.7 10.4 %dynamic_update_slice.9 = f32[3,512,512]{2,1,0:T(8,128)S(1)} dynamic-update-slice(f32[3,512,512]{2,1,0:T(8,128)S(1)} %broadcast_in_dim.2, f32[3,256,256]{2,1,0:T(8,128)} %slice_bitcast_fusion.2, s32[]{:T(128)} %constant.88.clone.1, s32[]{:T(128)S(6)} %select_n.65, s32[]{:T(128)S(6)} %select_n.66) | dynamic-update-slice | bytes 1572868 | tf_op jit(solution)/shard_map/dynamic_update_slice | solution.py:89
  115.1 2.3 fusion.39
  117.4 10.9 %dynamic_update_slice.10 = f32[3,512,512]{2,1,0:T(8,128)S(1)} dynamic-update-slice(f32[3,512,512]{2,1,0:T(8,128)S(1)} %dynamic_update_slice.9, f32[3,256,256]{2,1,0:T(8,128)} %fusion.39, s32[]{:T(128)} %constant.88.clone.1, s32[]{:T(128)S(6)} %select_n.67, s32[]{:T(128)S(6)} %select_n.68) | dynamic-update-slice | bytes 1572868 | tf_op jit(solution)/shard_map/dynamic_update_slice | solution.py:89
  128.2 2.3 fusion.38
  130.5 10.2 %dynamic_update_slice.11 = f32[3,512,512]{2,1,0:T(8,128)S(1)} dynamic-update-slice(f32[3,512,512]{2,1,0:T(8,128)S(1)} %dynamic_update_slice.10, f32[3,256,256]{2,1,0:T(8,128)} %fusion.38, s32[]{:T(128)} %constant.88.clone.1, s32[]{:T(128)S(6)} %select_n.69, s32[]{:T(128)S(6)} %select_n.70) | dynamic-update-slice | bytes 1572868 | tf_op jit(solution)/shard_map/dynamic_update_slice | solution.py:89
  140.8 0.2 slice.130
  141.0 7.9 %collective-permute-start.2 = (f32[3,512,256]{2,1,0:T(8,128)S(1)}, f32[3,512,256]{2,1,0:T(8,128)S(1)}, u32[]{:S(2)}, u32[]{:S(2)}) collective-permute-start(f32[3,512,256]{2,1,0:T(8,128)S(1)} %slice.130), channel_id=1, source_target_pairs={{0,4},{4,8},{8,12},{1,5},{5,9},{9,13},{2,6},{6,10},{10,14},{3,7},{... | collective-permute-start | bytes 4718600 | tf_op jit(solution)/shard_map/ppermute | solution.py:13
  148.8 34.4 %collective-permute-done.2 = f32[3,512,256]{2,1,0:T(8,128)S(1)} collective-permute-done((f32[3,512,256]{2,1,0:T(8,128)S(1)}, f32[3,512,256]{2,1,0:T(8,128)S(1)}, u32[]{:S(2)}, u32[]{:S(2)}) %collective-permute-start.2) | collective-permute-done | bytes 1572896 | tf_op jit(solution)/shard_map/ppermute | solution.py:13
  183.2 0.3 slice_add_fusion
  183.5 0.1 slice.132
  183.6 2.7 collective-permute-start.3
  186.3 1.0 pad_maximum_fusion.2
  187.4 0.9 multiply_reduce_fusion.2
  188.2 0.0 all-reduce.6.cloned.1.call-update
  188.3 0.0 copy-start.3
  188.3 0.0 all-reduce.4.cloned.1.call-start
  188.3 0.0 collective-permute-done.3
  188.3 2.2 slice_add_fusion.1
  190.5 0.0 all-reduce.4.cloned.1.call-update
  190.6 472.6 %all-reduce.6.cloned.1.call-done = (f32[2,2,256,256]{3,2,1,0:T(8,128)}, f32[256,256]{1,0:T(8,128)}) async-done(((f32[2,2,256,256]{3,2,1,0:T(8,128)}, f32[256,256]{1,0:T(8,128)}), (f32[2,2,256,256]{3,2,1,0:T(8,128)}, f32[256,256]{1,0:T(8,128)})) %all-reduce.6.cloned.1.call-update) | async-done | bytes 1310736 | tf_op jit(solution)/shard_map/psum | solution.py:101
  663.2 1.0 broadcast_add_fusion
  664.2 0.0 copy-start.6
  664.2 2.4 divide_add_fusion
  666.6 56.5 %all-reduce.4.cloned.1.call-done = f32[3,256,256]{2,1,0:T(8,128)} async-done(((f32[3,256,256]{2,1,0:T(8,128)}), f32[3,256,256]{2,1,0:T(8,128)}) %all-reduce.4.cloned.1.call-update) | async-done | bytes 786448 | tf_op jit(solution)/shard_map/psum | solution.py:98
  723.1 1.0 fusion.70
  724.1 1.9 fusion.66
  (17 shorter events, 0.0 us)
Async XLA Ops:
  7.2 17.3 %copy-start.10 = (s32[1,1,1,3,2]{3,4,2,1,0:T(2,128)S(1)}, s32[1,1,1,3,2]{3,4,2,1,0:T(2,128)}, u32[]{:S(2)}) copy-start(s32[1,1,1,3,2]{3,4,2,1,0:T(2,128)} %param.16) | copy-start | bytes 76
  7.2 29.9 %copy-start.2 = (f32[2,2,256,256]{3,2,1,0:T(8,128)S(1)}, f32[2,2,256,256]{3,2,1,0:T(8,128)}, u32[]{:S(2)}) copy-start(f32[2,2,256,256]{3,2,1,0:T(8,128)} %param.14) | copy-start | bytes 3145732
  7.2 656.0 %all-reduce.6.cloned.1.call-start = ((), (), s32[]{:S(2)}) async-start(), calls=%async_computation.1 | async-start | bytes 2621440 | tf_op jit(solution)/shard_map/psum | solution.py:101
  7.2 15.9 %collective-permute-start = (f32[2,256,256]{2,1,0:T(8,128)}, f32[2,256,256]{2,1,0:T(8,128)S(1)}, u32[]{:S(2)}, u32[]{:S(2)}) collective-permute-start(f32[2,256,256]{2,1,0:T(8,128)} %param.13), channel_id=1, source_target_pairs={{4,0},{8,4},{12,8},{5,1},{9,5},{13,9},{6,2},{10,6},{14,10},{7,3},{... | collective-permute-start | bytes 1572872 | tf_op jit(solution)/shard_map/ppermute | solution.py:13
  23.2 14.1 %collective-permute-start.1 = (f32[2,256,512]{2,1,0:T(8,128)S(1)}, f32[2,256,512]{2,1,0:T(8,128)S(1)}, u32[]{:S(2)}, u32[]{:S(2)}) collective-permute-start(f32[2,256,512]{2,1,0:T(8,128)S(1)} %constant_dynamic-update-slice_fusion), channel_id=1, source_target_pairs={{16,0},{32,16},{48,32},{64,48},{80,64},{96,80},{112,96},{128,112},... | collective-permute-start | bytes 3145736 | tf_op jit(solution)/shard_map/ppermute | solution.py:13
  38.3 1.1 copy-start
  65.8 3.8 copy-start.7
  102.6 1.7 copy-start.4
  141.0 42.3 %collective-permute-start.2 = (f32[3,512,256]{2,1,0:T(8,128)S(1)}, f32[3,512,256]{2,1,0:T(8,128)S(1)}, u32[]{:S(2)}, u32[]{:S(2)}) collective-permute-start(f32[3,512,256]{2,1,0:T(8,128)S(1)} %slice.130), channel_id=1, source_target_pairs={{0,4},{4,8},{8,12},{1,5},{5,9},{9,13},{2,6},{6,10},{10,14},{3,7},{... | collective-permute-start | bytes 4718600 | tf_op jit(solution)/shard_map/ppermute | solution.py:13
  183.2 3.1 copy-start.8
  183.2 3.1 copy-start.9
  183.5 3.9 copy-start.5
  183.5 3.9 copy-start.1
  183.6 4.7 collective-permute-start.3
  188.3 475.9 %copy-start.3 = (f32[2,2,256,256]{3,2,1,0:T(8,128)S(1)}, f32[2,2,256,256]{3,2,1,0:T(8,128)}, u32[]{:S(2)}) copy-start(f32[2,2,256,256]{3,2,1,0:T(8,128)} %param.14) | copy-start | bytes 3145732
  188.3 534.9 %all-reduce.4.cloned.1.call-start = ((), (), s32[]{:S(2)}) async-start(), calls=%async_computation | async-start | bytes 1572864 | tf_op jit(solution)/shard_map/psum | solution.py:98
  664.2 59.9 %copy-start.6 = (f32[2,256,256]{2,1,0:T(8,128)S(1)}, f32[2,256,256]{2,1,0:T(8,128)}, u32[]{:S(2)}) copy-start(f32[2,256,256]{2,1,0:T(8,128)} %param.13) | copy-start | bytes 1572868
Sparse Core Ops, SparseCore 0:
  188.4 474.7 all-reduce.5
  665.6 57.5 all-reduce.3
where the time goes:
time: 743 us; the launch traced here: 733 us
  waiting for transfers between devices  570 us (77%)
  matrix products  62.2 us (8%)
  local copies, waits for them, and re-layouts  36.8 us (5%)
  between operations  26.6 us (4%)
  starting transfers between devices  19.9 us (3%)
  other arithmetic  17.1 us (2%)
    psum x1, waiting for transfers between devices, on_device(): lax.psum((jnp.stack([numer_real, numer_imag]), density), ('tile', 'band',...  473 us
    psum x1, waiting for transfers between devices, on_device(): tile_total = lax.psum(tile_core, 'pos')  56.5 us
    ppermute x4, waiting for transfers between devices, shifted(): return lax.ppermute(block, axis, route)  41.2 us
    dynamic_update_slice x3, local copies, waits for them, and re-layouts, on_device(): lax.dynamic_update_slice(running, previous + contributions[number], corne...  31.5 us
    ppermute x4, starting transfers between devices, shifted(): return lax.ppermute(block, axis, route)  19.8 us
  transfers between devices with their start and end apart: 6, of which 4 were waited for; matrix products, arithmetic and copies ran while one was open for 1% of the time, Pallas kernels for 0%

commit v1 on v0

--- a/solution.py
+++ b/solution.py
@@ -95,7 +95,7 @@
     column_core = running[:, :, :tile_cols].at[:, :, :pixels].add(from_left)
     from_above = shifted(column_core[:, tile_rows:, :], "tile", 1)
     tile_core = column_core[:, :tile_rows, :].at[:, :pixels, :].add(from_above)
-    tile_total = lax.psum(tile_core, "pos")
+    tile_total = jnp.sum(lax.all_gather(tile_core, "pos"), axis=0)
     tile_light = tile_total[2]
     object_new = object_planes + tile_total[:2] / (tile_light + 1.0)
     sum_numer, sum_density = lax.psum(

time: 743 us -> 691 us (0.930)
  the two profiles are of different devices: /device:TPU:2 before, /device:TPU:1 now
where the time goes in v1:
time: 691 us; the launch traced here: 681 us
  waiting for transfers between devices  517 us (75%)
  matrix products  62.2 us (9%)
  local copies, waits for them, and re-layouts  38.5 us (6%)
  between operations  28 us (4%)
  starting transfers between devices  18.6 us (3%)
  other arithmetic  17.2 us (2%)
    psum x1, waiting for transfers between devices, on_device(): lax.psum((jnp.stack([numer_real, numer_imag]), density), ('tile', 'band',...  469 us
    ppermute x4, waiting for transfers between devices, shifted(): return lax.ppermute(block, axis, route)  48.3 us
    dynamic_update_slice x3, local copies, waits for them, and re-layouts, on_device(): lax.dynamic_update_slice(running, previous + contributions[number], corne...  33.2 us
    ppermute x4, starting transfers between devices, shifted(): return lax.ppermute(block, axis, route)  18.5 us
  transfers between devices with their start and end apart: 6, of which 5 were waited for; matrix products, arithmetic and copies ran while one was open for 1% of the time, Pallas kernels for 0%

profile of v1, /device:TPU:1, one launch (start us, length us, event | category | flops | bytes accessed | tf_op | source)
XLA Modules:
  0.0 681.4 jit_solution(3185693564247416034)
XLA Ops:
  8.0 0.0 copy-start.10
  8.0 0.0 copy-start.2
  8.0 0.0 all-reduce.3.cloned.1.call-start
  8.1 1.4 collective-permute-start
  9.5 1.1 constant_dynamic-update-slice_fusion.1
  10.6 8.3 %collective-permute-done = f32[2,256,256]{2,1,0:T(8,128)S(1)} collective-permute-done((f32[2,256,256]{2,1,0:T(8,128)}, f32[2,256,256]{2,1,0:T(8,128)S(1)}, u32[]{:S(2)}, u32[]{:S(2)}) %collective-permute-start) | collective-permute-done | bytes 524320 | tf_op jit(solution)/shard_map/ppermute | solution.py:13
  18.9 0.1 constant_dynamic-update-slice_fusion
  19.0 9.3 %collective-permute-start.1 = (f32[2,256,512]{2,1,0:T(8,128)S(1)}, f32[2,256,512]{2,1,0:T(8,128)S(1)}, u32[]{:S(2)}, u32[]{:S(2)}) collective-permute-start(f32[2,256,512]{2,1,0:T(8,128)S(1)} %constant_dynamic-update-slice_fusion), channel_id=1, source_target_pairs={{16,0},{32,16},{48,32},{64,48},{80,64},{96,80},{112,96},{128,112},... | collective-permute-start | bytes 3145736 | tf_op jit(solution)/shard_map/ppermute | solution.py:13
  28.3 0.6 fusion.170
  41.0 0.1 add_reduce_fusion.2
  41.0 0.1 slice_bitcast_fusion.6
  41.1 0.3 collective-permute-done.1
  41.4 1.0 fusion.63
  42.4 0.1 pad_maximum_fusion.1
  42.5 0.1 slice_bitcast_fusion.4
  42.6 1.0 copy-done
  43.6 3.7 fusion.16
  47.3 3.7 fusion.31
  51.1 4.1 fusion.8
  55.1 3.6 fusion.10
  58.7 3.7 fusion.17
  62.4 3.7 fusion.30
  66.2 3.8 fusion.20
  70.0 0.0 copy-start.7
  70.0 3.8 add_reduce_fusion.1
  73.8 0.3 bitcast_multiply_fusion.2
  74.1 3.6 fusion.36
  77.7 3.8 fusion.32
  81.5 3.6 multiply_subtract_fusion
  85.1 3.6 fusion
  88.7 4.0 fusion.2
  92.7 3.6 multiply_add_fusion
  96.4 3.9 add_subtract_fusion
  100.3 6.0 multiply_reduce_fusion.1
  106.3 0.3 bitcast_multiply_fusion.1
  106.6 0.2 pad_maximum_fusion
  106.7 1.0 slice_bitcast_fusion.2
  107.7 0.7 copy-done.4
  108.4 0.4 broadcast_in_dim.2
  108.8 10.9 %dynamic_update_slice.9 = f32[3,512,512]{2,1,0:T(8,128)S(1)} dynamic-update-slice(f32[3,512,512]{2,1,0:T(8,128)S(1)} %broadcast_in_dim.2, f32[3,256,256]{2,1,0:T(8,128)} %slice_bitcast_fusion.2, s32[]{:T(128)} %constant.88.clone.1, s32[]{:T(128)S(6)} %select_n.65, s32[]{:T(128)S(6)} %select_n.66) | dynamic-update-slice | bytes 1572868 | tf_op jit(solution)/shard_map/dynamic_update_slice | solution.py:89
  119.7 2.3 fusion.39
  122.0 10.2 %dynamic_update_slice.10 = f32[3,512,512]{2,1,0:T(8,128)S(1)} dynamic-update-slice(f32[3,512,512]{2,1,0:T(8,128)S(1)} %dynamic_update_slice.9, f32[3,256,256]{2,1,0:T(8,128)} %fusion.39, s32[]{:T(128)} %constant.88.clone.1, s32[]{:T(128)S(6)} %select_n.67, s32[]{:T(128)S(6)} %select_n.68) | dynamic-update-slice | bytes 1572868 | tf_op jit(solution)/shard_map/dynamic_update_slice | solution.py:89
  132.2 2.3 fusion.38
  134.5 12.1 %dynamic_update_slice.11 = f32[3,512,512]{2,1,0:T(8,128)S(1)} dynamic-update-slice(f32[3,512,512]{2,1,0:T(8,128)S(1)} %dynamic_update_slice.10, f32[3,256,256]{2,1,0:T(8,128)} %fusion.38, s32[]{:T(128)} %constant.88.clone.1, s32[]{:T(128)S(6)} %select_n.69, s32[]{:T(128)S(6)} %select_n.70) | dynamic-update-slice | bytes 1572868 | tf_op jit(solution)/shard_map/dynamic_update_slice | solution.py:89
  146.6 0.2 slice.130
  146.8 1.8 collective-permute-start.2
  148.6 32.8 %collective-permute-done.2 = f32[3,512,256]{2,1,0:T(8,128)S(1)} collective-permute-done((f32[3,512,256]{2,1,0:T(8,128)S(1)}, f32[3,512,256]{2,1,0:T(8,128)S(1)}, u32[]{:S(2)}, u32[]{:S(2)}) %collective-permute-start.2) | collective-permute-done | bytes 1572896 | tf_op jit(solution)/shard_map/ppermute | solution.py:13
  181.3 0.3 slice_add_fusion
  181.6 0.1 slice.132
  181.7 6.0 collective-permute-start.3
  187.7 1.0 pad_maximum_fusion.2
  188.8 0.0 copy-done.1
  188.8 0.9 multiply_reduce_fusion.2
  189.6 0.0 all-reduce.3.cloned.1.call-update
  189.6 0.0 copy-start.3
  189.6 0.0 all-gather.3.cloned.1.call-start
  189.7 6.9 %collective-permute-done.3 = f32[3,256,256]{2,1,0:T(8,128)S(1)} collective-permute-done((f32[3,256,256]{2,1,0:T(8,128)S(1)}, f32[3,256,256]{2,1,0:T(8,128)S(1)}, u32[]{:S(2)}, u32[]{:S(2)}) %collective-permute-start.3) | collective-permute-done | bytes 786464 | tf_op jit(solution)/shard_map/ppermute | solution.py:13
  196.6 2.1 slice_add_fusion.1
  198.7 0.0 all-gather.3.cloned.1.call-update
  198.7 468.5 %all-reduce.3.cloned.1.call-done = (f32[2,2,256,256]{3,2,1,0:T(8,128)}, f32[256,256]{1,0:T(8,128)}) async-done(((f32[2,2,256,256]{3,2,1,0:T(8,128)}, f32[256,256]{1,0:T(8,128)}), (f32[2,2,256,256]{3,2,1,0:T(8,128)}, f32[256,256]{1,0:T(8,128)})) %all-reduce.3.cloned.1.call-update) | async-done | bytes 1310736 | tf_op jit(solution)/shard_map/psum | solution.py:101
  667.2 1.0 broadcast_add_fusion
  668.2 2.4 divide_add_fusion
  670.6 2.2 reduce_sum.82
  672.9 0.9 fusion.66
  (18 shorter events, 0.1 us)
Async XLA Ops:
  8.0 20.3 %copy-start.10 = (s32[1,1,1,3,2]{3,4,2,1,0:T(2,128)S(1)}, s32[1,1,1,3,2]{3,4,2,1,0:T(2,128)}, u32[]{:S(2)}) copy-start(s32[1,1,1,3,2]{3,4,2,1,0:T(2,128)} %param.16) | copy-start | bytes 76
  8.0 32.9 %copy-start.2 = (f32[2,2,256,256]{3,2,1,0:T(8,128)S(1)}, f32[2,2,256,256]{3,2,1,0:T(8,128)}, u32[]{:S(2)}) copy-start(f32[2,2,256,256]{3,2,1,0:T(8,128)} %param.14) | copy-start | bytes 3145732
  8.0 659.2 %all-reduce.3.cloned.1.call-start = ((), (), s32[]{:S(2)}) async-start(), calls=%async_computation.1 | async-start | bytes 2621440 | tf_op jit(solution)/shard_map/psum | solution.py:101
  8.1 10.9 %collective-permute-start = (f32[2,256,256]{2,1,0:T(8,128)}, f32[2,256,256]{2,1,0:T(8,128)S(1)}, u32[]{:S(2)}, u32[]{:S(2)}) collective-permute-start(f32[2,256,256]{2,1,0:T(8,128)} %param.13), channel_id=1, source_target_pairs={{4,0},{8,4},{12,8},{5,1},{9,5},{13,9},{6,2},{10,6},{14,10},{7,3},{... | collective-permute-start | bytes 1572872 | tf_op jit(solution)/shard_map/ppermute | solution.py:13
  19.0 22.5 %collective-permute-start.1 = (f32[2,256,512]{2,1,0:T(8,128)S(1)}, f32[2,256,512]{2,1,0:T(8,128)S(1)}, u32[]{:S(2)}, u32[]{:S(2)}) collective-permute-start(f32[2,256,512]{2,1,0:T(8,128)S(1)} %constant_dynamic-update-slice_fusion), channel_id=1, source_target_pairs={{16,0},{32,16},{48,32},{64,48},{80,64},{96,80},{112,96},{128,112},... | collective-permute-start | bytes 3145736 | tf_op jit(solution)/shard_map/ppermute | solution.py:13
  42.5 1.1 copy-start
  70.0 3.8 copy-start.7
  106.7 1.7 copy-start.4
  146.8 34.5 %collective-permute-start.2 = (f32[3,512,256]{2,1,0:T(8,128)S(1)}, f32[3,512,256]{2,1,0:T(8,128)S(1)}, u32[]{:S(2)}, u32[]{:S(2)}) collective-permute-start(f32[3,512,256]{2,1,0:T(8,128)S(1)} %slice.130), channel_id=1, source_target_pairs={{0,4},{4,8},{8,12},{1,5},{5,9},{9,13},{2,6},{6,10},{10,14},{3,7},{... | collective-permute-start | bytes 4718600 | tf_op jit(solution)/shard_map/ppermute | solution.py:13
  181.3 6.4 copy-start.8
  181.3 6.4 copy-start.9
  181.6 7.1 %copy-start.5 = (f32[3,512,256]{2,1,0:T(8,128)}, f32[3,512,256]{2,1,0:T(8,128)S(1)}, u32[]{:S(2)}) copy-start(f32[3,512,256]{2,1,0:T(8,128)S(1)} %slice_add_fusion) | copy-start | bytes 4718596
  181.6 7.1 %copy-start.1 = (f32[3,2,256,256]{3,2,0,1:T(8,128)S(1)}, f32[3,2,256,256]{3,2,0,1:T(8,128)}, u32[]{:S(2)}) copy-start(f32[3,2,256,256]{3,2,0,1:T(8,128)} %copy-done) | copy-start | bytes 4718596
  181.7 14.9 %collective-permute-start.3 = (f32[3,256,256]{2,1,0:T(8,128)S(1)}, f32[3,256,256]{2,1,0:T(8,128)S(1)}, u32[]{:S(2)}, u32[]{:S(2)}) collective-permute-start(f32[3,256,256]{2,1,0:T(8,128)S(1)} %slice.132), channel_id=1, source_target_pairs={{0,16},{16,32},{32,48},{48,64},{64,80},{80,96},{96,112},{112,128},... | collective-permute-start | bytes 2359304 | tf_op jit(solution)/shard_map/ppermute | solution.py:13
  189.6 478.6 %copy-start.3 = (f32[2,2,256,256]{3,2,1,0:T(8,128)S(1)}, f32[2,2,256,256]{3,2,1,0:T(8,128)}, u32[]{:S(2)}) copy-start(f32[2,2,256,256]{3,2,1,0:T(8,128)} %param.14) | copy-start | bytes 3145732
  189.6 480.9 %all-gather.3.cloned.1.call-start = ((), (), s32[]{:S(2)}) async-start(), calls=%async_computation | async-start | bytes 3932160 | tf_op jit(solution)/shard_map/all_gather | solution.py:98
  670.6 2.3 copy-start.6
Sparse Core Ops, SparseCore 0:
  189.8 477.4 all-reduce.2
Sparse Core Ops, SparseCore 1:
  198.8 58.4 all-gather.2
